TPU v7x, 512 devices: a whole 4x8x8 slice. The times are simulated.
512 devices in a mesh: dp: 32 (over x, z_hi, core), mp: 16 (over z_lo, y).
Axes of the slice: x: 4, y: 8, z: 8 (z_hi: 4, z_lo: 2; z = z_hi * 2 + z_lo), core: 2. Of those that a mesh axis runs over, the one named last changes fastest.
Arguments:
- img_tokens: bfloat16 [512, 128, 1408], P(('dp', 'mp')), may hold values from -6 to 6
- w_key: bfloat16 [1408, 2048], P(None, 'mp'), may hold values from -0.15625 to 0.15625
- w_value: bfloat16 [1408, 2048], P(None, 'mp'), may hold values from -0.15625 to 0.15625
- queries: bfloat16 [512, 32, 2048], P('dp', None, 'mp'), may hold values from -6 to 6
- lengths: int32 [512], P('dp'), may hold values from 1 to 32
- d_out: bfloat16 [512, 32, 2048], P('dp', None, 'mp'), may hold values from -6 to 6
- img_pooled: bfloat16 [512, 1408], P(('dp', 'mp')), may hold values from -40 to 40
- w_proj: bfloat16 [1408, 2048], P(None, 'mp'), may hold values from -0.19921875 to 0.19921875
- txt_embed: bfloat16 [512, 2048], P('dp', 'mp'), may hold values from -80 to 80
- inv_temp: float32 [1], replicated, may hold values from 30 to 100
Outputs:
- attended: bfloat16 [512, 32, 2048], P('dp', None, 'mp')
- grad_queries: bfloat16 [512, 32, 2048], P('dp', None, 'mp')
- dw_key: float32 [1408, 2048], P('dp', 'mp')
- dw_value: float32 [1408, 2048], P('dp', 'mp')
- contrast: float32 [2, 512], P(None, 'dp')
Inputs may be any that keep to these rules, and one draw needn't show every extreme that they name: lengths: each caption's count of real positions.
All inputs are finite; a program needn't handle non-finite values.
Results may differ from a plain program's by a relative error of at most 0.0081.
Values may be sent and summed in bfloat16 or wider, within the bound.
A program may use at most 64 MiB of HBM per device.

v0:
```python
import jax
import jax.numpy as jnp
from jax import lax
from jax.sharding import PartitionSpec as P

HD = 128


def project_pairs(tokens, w_pair):
    count = tokens.shape[0]
    flat = tokens.reshape(count * tokens.shape[1], tokens.shape[2])
    result = jnp.dot(flat, w_pair, preferred_element_type=jnp.float32)
    return result.astype(jnp.bfloat16).reshape(count, tokens.shape[1], w_pair.shape[1])


def weight_terms(tokens, grad_pairs):
    flat_tokens = tokens.reshape(-1, tokens.shape[2])
    flat_grads = grad_pairs.reshape(-1, grad_pairs.shape[2])
    return jnp.einsum("rc,re->ce", flat_tokens, flat_grads, preferred_element_type=jnp.float32)


def pair_dots(left, right):
    return jnp.einsum("ic,jc->ij", left, right, preferred_element_type=jnp.float32)


def squares(matrix):
    return jnp.sum(jnp.square(matrix.astype(jnp.float32)), axis=1)


def body(
    img_tokens, w_key, w_value, queries, lengths, d_out, img_pooled, w_proj, txt_embed, inv_temp
):
    width_here = w_key.shape[1]
    heads_here = width_here // HD
    w_pair = jnp.concatenate([w_key, w_value], axis=1)
    all_tokens = lax.all_gather(img_tokens, "mp", axis=0, tiled=True)
    kv_pairs = project_pairs(all_tokens, w_pair)
    captions = queries.shape[0]
    caption_len = queries.shape[1]
    image_len = kv_pairs.shape[1]
    inv_root = HD ** (-0.5)
    key_heads = kv_pairs[:, :, :width_here].reshape(captions, image_len, heads_here, HD)
    value_heads = kv_pairs[:, :, width_here:].reshape(captions, image_len, heads_here, HD)
    query_heads = queries.reshape(captions, caption_len, heads_here, HD)
    scores = (
        jnp.einsum("blhd,bthd->bhlt", query_heads, key_heads, preferred_element_type=jnp.float32)
        * inv_root
    )
    probs = jax.nn.softmax(scores, axis=-1)
    probs_b = probs.astype(jnp.bfloat16)
    keep_rows = (jnp.arange(caption_len)[None, :] < lengths[:, None]).astype(jnp.float32)
    output = jnp.einsum("bhlt,bthd->blhd", probs_b, value_heads, preferred_element_type=jnp.float32)
    attended = (
        (output * keep_rows[:, :, None, None])
        .reshape(captions, caption_len, width_here)
        .astype(jnp.bfloat16)
    )
    masked = (d_out.astype(jnp.float32) * keep_rows[:, :, None]).astype(jnp.bfloat16)
    grad_heads = masked.reshape(captions, caption_len, heads_here, HD)
    grad_values = jnp.einsum(
        "bhlt,blhd->bthd", probs_b, grad_heads, preferred_element_type=jnp.float32
    ).astype(jnp.bfloat16)
    grad_probs = jnp.einsum(
        "blhd,bthd->bhlt", grad_heads, value_heads, preferred_element_type=jnp.float32
    )
    row_dots = jnp.sum(probs * grad_probs, axis=-1, keepdims=True)
    grad_scores = (probs * (grad_probs - row_dots) * inv_root).astype(jnp.bfloat16)
    grad_queries = jnp.einsum(
        "bhlt,bthd->blhd", grad_scores, key_heads, preferred_element_type=jnp.float32
    )
    grad_queries = grad_queries.reshape(captions, caption_len, width_here).astype(jnp.bfloat16)
    grad_keys = jnp.einsum(
        "bhlt,blhd->bthd", grad_scores, query_heads, preferred_element_type=jnp.float32
    ).astype(jnp.bfloat16)
    grad_pairs = jnp.concatenate(
        [
            grad_keys.reshape(captions, image_len, width_here),
            grad_values.reshape(captions, image_len, width_here),
        ],
        axis=2,
    )
    weight_sums = weight_terms(all_tokens, grad_pairs)
    shares = lax.psum_scatter(weight_sums, "dp", scatter_dimension=0, tiled=True)
    dw_key = shares[:, :width_here]
    dw_value = shares[:, width_here:]
    pooled_group = lax.all_gather(img_pooled, "mp", axis=0, tiled=True)
    img_part = jnp.dot(pooled_group, w_proj, preferred_element_type=jnp.float32).astype(
        jnp.bfloat16
    )
    offset_rows = lax.axis_index("dp") * captions
    img_group, txt_group = (
        lax.all_gather(img_part, "mp", axis=1, tiled=True),
        lax.all_gather(txt_embed, "mp", axis=1, tiled=True),
    )
    img_every, txt_every = (
        lax.all_gather(img_group, "dp", axis=0, tiled=True),
        lax.all_gather(txt_group, "dp", axis=0, tiled=True),
    )
    img_sq_all = squares(img_every)
    txt_sq_all = squares(txt_every)
    dots_image = pair_dots(img_group, txt_every)
    dots_caption = pair_dots(txt_group, img_every)
    img_sq_here = lax.dynamic_slice_in_dim(img_sq_all, offset_rows, captions, 0)
    txt_sq_here = lax.dynamic_slice_in_dim(txt_sq_all, offset_rows, captions, 0)
    logits_image = (
        inv_temp[0]
        * dots_image
        * lax.rsqrt(img_sq_here + 1e-06)[:, None]
        * lax.rsqrt(txt_sq_all + 1e-06)[None, :]
    )
    logits_caption = (
        inv_temp[0]
        * dots_caption
        * lax.rsqrt(txt_sq_here + 1e-06)[:, None]
        * lax.rsqrt(img_sq_all + 1e-06)[None, :]
    )
    diag_image = jnp.diagonal(lax.dynamic_slice_in_dim(logits_image, offset_rows, captions, 1))
    diag_caption = jnp.diagonal(lax.dynamic_slice_in_dim(logits_caption, offset_rows, captions, 1))
    image_side = jax.nn.logsumexp(logits_image, axis=1) - diag_image
    caption_side = jax.nn.logsumexp(logits_caption, axis=1) - diag_caption
    contrast = jnp.stack([image_side, caption_side])
    return (attended, grad_queries, dw_key, dw_value, contrast)


def solution(mesh):
    placed = (
        P(("dp", "mp"), None, None),
        P(None, "mp"),
        P(None, "mp"),
        P("dp", None, "mp"),
        P("dp"),
        P("dp", None, "mp"),
        P(("dp", "mp"), None),
        P(None, "mp"),
        P("dp", "mp"),
        P(),
    )
    return jax.shard_map(
        body,
        mesh=mesh,
        in_specs=placed,
        out_specs=(
            P("dp", None, "mp"),
            P("dp", None, "mp"),
            P("dp", "mp"),
            P("dp", "mp"),
            P(None, "dp"),
        ),
        check_vma=False,
    )
```

profile of v0, /device:TPU:1, one launch (start us, length us, event | category | flops | bytes accessed | tf_op | source)
XLA Modules:
  0.0 595.4 jit_solution(7347652347336421673)
XLA Ops:
  7.2 0.0 copy-start
  7.2 0.0 all-gather.9.cloned.1.call-start
  7.2 29.2 %all-gather = bf16[16,1,1408]{2,1,0:T(2,128)(2,1)S(1)} all-gather(bf16[1,1,1408]{2,1,0:T(2,128)(2,1)} %bitcast.76), channel_id=1, replica_groups=mesh['dp'=32,'mp'=16] {'mp'}, dimensions={0}, use_global_device_ids=true | all-gather | bytes 47872 | tf_op jit(solution)/shard_map/all_gather | solution.py:86
  36.4 0.0 copy-done
  36.5 0.2 convolution_convert_fusion.4
  36.6 25.2 %all_gather.20 = bf16[16,2048]{1,0:T(8,128)(2,1)} all-gather(bf16[16,128]{1,0:T(8,128)(2,1)S(1)} %convolution_convert_fusion.4), channel_id=1, replica_groups=mesh['dp'=32,'mp'=16] {'mp'}, dimensions={1}, use_global_device_ids=true | all-gather | bytes 69632 | tf_op jit(solution)/shard_map/all_gather | solution.py:92
  61.8 0.0 all-gather.9.cloned.1.call-update
  61.9 0.0 all-gather.7.cloned.1.call-start
  61.9 27.5 %all_gather.21 = bf16[16,2048]{1,0:T(8,128)(2,1)} all-gather(bf16[16,128]{1,0:T(8,128)(2,1)} %param.18), channel_id=1, replica_groups=mesh['dp'=32,'mp'=16] {'mp'}, dimensions={1}, use_global_device_ids=true | all-gather | bytes 69632 | tf_op jit(solution)/shard_map/all_gather | solution.py:93
  89.4 0.0 all-gather.7.cloned.1.call-update
  89.4 0.0 all-gather.5.cloned.1.call-start
  89.5 0.7 all-gather.5.cloned.1.call-update
  90.1 0.0 all-reduce.3.cloned.1.call-start
  90.8 1.3 dynamic-slice.4
  92.8 0.7 fusion.40
  93.5 0.0 copy-start.2
  93.5 43.3 %all-gather.9.cloned.1.call-done = bf16[512,2048]{1,0:T(8,128)(2,1)} async-done(((bf16[16,2048]{1,0:T(8,128)(2,1)}), bf16[512,2048]{1,0:T(8,128)(2,1)}) %all-gather.9.cloned.1.call-update) | async-done | bytes 2097168 | tf_op jit(solution)/shard_map/all_gather | solution.py:96
  136.9 2.1 multiply_reduce_fusion.1
  138.9 0.1 add_rsqrt_fusion.3
  139.0 0.0 copy-start.1
  139.0 0.0 copy-start.3
  139.0 58.6 %all-gather.7.cloned.1.call-done = bf16[512,2048]{1,0:T(8,128)(2,1)} async-done(((bf16[16,2048]{1,0:T(8,128)(2,1)}), bf16[512,2048]{1,0:T(8,128)(2,1)}) %all-gather.7.cloned.1.call-update) | async-done | bytes 2097168 | tf_op jit(solution)/shard_map/all_gather | solution.py:97
  197.7 2.1 multiply_reduce_fusion
  199.7 0.1 add_rsqrt_fusion.2
  199.8 0.0 copy-done.2
  199.8 0.0 copy-start.6
  199.8 2.4 fusion.54
  202.2 0.1 constant_dynamic-slice_fusion
  202.3 0.0 copy-done.1
  202.3 0.0 copy-done.3
  202.3 0.8 fusion.53
  203.1 69.8 %all-gather.5.cloned.1.call-done = bf16[16,128,1408]{2,1,0:T(8,128)(2,1)} async-done(((bf16[1,128,1408]{2,1,0:T(8,128)(2,1)}), bf16[16,128,1408]{2,1,0:T(8,128)(2,1)}) %all-gather.5.cloned.1.call-update) | async-done | bytes 5767184 | tf_op jit(solution)/shard_map/all_gather | solution.py:36
  272.9 0.0 copy-done.6
  272.9 4.6 fusion.2
  277.6 0.0 copy-start.5
  277.6 0.0 copy-start.4
  277.6 0.5 copy.29
  278.1 0.4 copy-done.5
  278.5 0.4 fusion.9
  278.8 2.7 fusion.52
  281.6 0.0 copy-done.4
  281.6 0.4 fusion.29
  282.0 1.5 fusion.3
  283.5 3.8 convolution_convert_fusion.2
  287.3 5.7 convolution_bitcast_fusion
  293.0 0.0 all-reduce.3.cloned.1.call-update
  293.1 0.1 dynamic-slice_bitcast_fusion
  293.1 0.7 gather_fusion
  293.8 0.7 gather_fusion.1
  294.5 0.2 exponential_reduce_fusion.1
  294.7 0.2 exponential_reduce_fusion
  294.9 0.6 pad_maximum_fusion
  295.5 1.6 fusion.14
  297.1 3.1 fusion.13
  300.2 286.2 %all-reduce.3.cloned.1.call-done = f32[1408,256]{0,1:T(8,128)} async-done(((f32[1408,256]{0,1:T(8,128)}), f32[1408,256]{0,1:T(8,128)}) %all-reduce.3.cloned.1.call-update) | async-done | bytes 1441808
  586.4 1.1 fusion.51
  587.5 0.7 copy.25
  588.2 0.7 copy.26
  (6 shorter events, 0.0 us)
Async XLA Ops:
  7.2 29.3 %copy-start = (bf16[1408,128]{1,0:T(8,128)(2,1)S(1)}, bf16[1408,128]{1,0:T(8,128)(2,1)}, u32[]{:S(2)}) copy-start(bf16[1408,128]{1,0:T(8,128)(2,1)} %param.17) | copy-start | bytes 1081348
  7.2 129.7 %all-gather.9.cloned.1.call-start = ((), (), s32[]{:S(2)}) async-start(), calls=%async_computation.2 | async-start | bytes 2162688 | tf_op jit(solution)/shard_map/all_gather | solution.py:96
  61.9 135.8 %all-gather.7.cloned.1.call-start = ((), (), s32[]{:S(2)}) async-start(), calls=%async_computation.1 | async-start | bytes 2162688 | tf_op jit(solution)/shard_map/all_gather | solution.py:97
  89.4 183.5 %all-gather.5.cloned.1.call-start = ((), (), s32[]{:S(2)}) async-start(), calls=%async_computation | async-start | bytes 6127616 | tf_op jit(solution)/shard_map/all_gather | solution.py:36
  90.1 496.3 %all-reduce.3.cloned.1.call-start = ((), (), s32[]{:S(2)}) async-start(), calls=%async_computation.3 | async-start | bytes 2883584
  93.5 106.3 %copy-start.2 = (bf16[16,2048]{1,0:T(8,128)(2,1)S(1)}, bf16[16,2048]{1,0:T(8,128)(2,1)}, u32[]{:S(2)}) copy-start(bf16[16,2048]{1,0:T(8,128)(2,1)} %all_gather.20) | copy-start | bytes 196612
  139.0 63.3 %copy-start.1 = (bf16[512,2048]{1,0:T(8,128)(2,1)S(1)}, bf16[512,2048]{1,0:T(8,128)(2,1)}, u32[]{:S(2)}) copy-start(bf16[512,2048]{1,0:T(8,128)(2,1)} %all-gather.9.cloned.1.call-done) | copy-start | bytes 6291460
  139.0 63.3 %copy-start.3 = (bf16[16,2048]{1,0:T(8,128)(2,1)S(1)}, bf16[16,2048]{1,0:T(8,128)(2,1)}, u32[]{:S(2)}) copy-start(bf16[16,2048]{1,0:T(8,128)(2,1)} %all_gather.21) | copy-start | bytes 196612
  199.8 73.1 %copy-start.6 = (bf16[1408,128]{1,0:T(8,128)(2,1)S(1)}, bf16[1408,128]{1,0:T(8,128)(2,1)}, u32[]{:S(2)}) copy-start(bf16[1408,128]{1,0:T(8,128)(2,1)} %param.12) | copy-start | bytes 1081348
  277.6 0.9 copy-start.5
  277.6 4.0 copy-start.4
Sparse Core Ops, SparseCore 0:
  62.0 74.8 all-gather.8
  140.0 57.6 all-gather.6
  199.7 73.1 all-gather.4
  293.2 293.1 all-reduce.2
where the time goes:
time: 596 us; the launch traced here: 595 us
  waiting for transfers between devices  459 us (77%)
  blocking collectives  81.9 us (14%)
  matrix products  24.5 us (4%)
  between operations  15.2 us (3%)
  other arithmetic  8.74 us (1%)
  local copies, waits for them, and re-layouts  6.12 us (1%)
    unnamed x5, waiting for transfers between devices  287 us
    all_gather x1, waiting for transfers between devices, body(): all_tokens = lax.all_gather(img_tokens, 'mp', axis=0, tiled=True)  69.8 us
    all_gather x1, waiting for transfers between devices, body(): lax.all_gather(txt_group, 'dp', axis=0, tiled=True)  58.6 us
    all_gather x1, waiting for transfers between devices, body(): lax.all_gather(img_group, 'dp', axis=0, tiled=True)  43.3 us
    all_gather x1, blocking collectives, body(): pooled_group = lax.all_gather(img_pooled, 'mp', axis=0, tiled=True)  29.2 us
    all_gather x1, blocking collectives, body(): lax.all_gather(txt_embed, 'mp', axis=1, tiled=True)  27.5 us
    all_gather x1, blocking collectives, body(): lax.all_gather(img_part, 'mp', axis=1, tiled=True)  25.2 us
  transfers between devices with their start and end apart: 4, of which 4 were waited for; matrix products, arithmetic and copies ran while one was open for 3% of the time, Pallas kernels for 0%

commit v1 on v0

v1 whole, which is shorter than its diff:
```python
import functools

import jax
import jax.numpy as jnp
from jax import lax
from jax.experimental import pallas as pl
from jax.experimental.pallas import tpu as pltpu
from jax.sharding import PartitionSpec as P

HD = 128
NX, NZH, NC, NZL, NY = 4, 4, 2, 2, 8
DI = 1408
ROOT = HD ** (-0.5)
MESH = pl.DeviceIdType.MESH
F32 = jnp.float32
BF16 = jnp.bfloat16


def nt(a, b):
    return lax.dot_general(a, b, (((1,), (1,)), ((), ())), preferred_element_type=F32)


def tn(a, b):
    return lax.dot_general(a, b, (((0,), (0,)), ((), ())), preferred_element_type=F32)


def nn(a, b):
    return jnp.dot(a, b, preferred_element_type=F32)


def kernel(
    tok, wk, wv, q, length, do, pooled, wp, txt, temp,
    att, gq, dwk, dwv, con,
    ring, w, qp, dop, att_s, gq_s, att_r, gq_r, acc,
    s1, r1, own2, s2, r2, s3, r3, t3, s4, r4, s5, r5,
    prow, gbuf, pk, rk, zs, zr, cs, cr,
    ring_ss, ring_rs, z_ss, z_rs, w_ss, w_rs, c1_ss, c1_rs, c2_ss, c2_rs, c3_ss, c3_rs,
    c4_ss, c4_rs, c5_ss, c5_rs, c6_ss, c6_rs, t1_ss, t1_rs, t2_ss, t2_rs, t3_ss, t3_rs,
    t4_ss, t4_rs, t5_ss, t5_rs,
):
    d = lax.axis_index("dp")
    m = lax.axis_index("mp")
    x, zh, c = d // (NZH * NC), lax.rem(d // NC, NZH), lax.rem(d, NC)
    zl, y = m // NY, lax.rem(m, NY)

    def y_at(k):
        return lax.rem(y + k + NY, NY)

    def y_peer(k):
        return (d, zl * NY + y_at(k))

    def x_at(k):
        return lax.rem(x + k, NX)

    def x_peer(k):
        return (x_at(k) * (NZH * NC) + zh * NC + c, m)

    def h_at(k):
        return lax.rem(zh + k, NZH)

    def h_peer(k):
        return (x * (NZH * NC) + h_at(k) * NC + c, m)

    z_peer = (d, (1 - zl) * NY + y)
    c_peer = (d + 1 - 2 * c, m)

    def remote(src, dst, ss, rs, to):
        return pltpu.make_async_remote_copy(
            src_ref=src, dst_ref=dst, send_sem=ss, recv_sem=rs, device_id=to, device_id_type=MESH
        )

    sent = []

    def send(copy):
        copy.start()
        sent.append(copy)
        return copy

    barrier = pltpu.get_barrier_semaphore()
    peers = [y_peer(k) for k in range(1, NY)] + [z_peer, c_peer]
    peers += [x_peer(k) for k in range(1, NX)] + [h_peer(k) for k in range(1, NZH)]
    for peer in peers:
        pl.semaphore_signal(barrier, inc=1, device_id=peer, device_id_type=MESH)

    w[0, :, 0:HD] = wk[...]
    w[1, :, 0:HD] = wv[...]
    row = jnp.zeros((16, 128), F32)
    rows = lax.broadcasted_iota(jnp.int32, (16, 128), 0)
    for i in range(DI // 128):
        piece = pooled[0:1, i * 128 : (i + 1) * 128].astype(F32)
        row = jnp.where(rows == i, piece, row)
    prow[zl, y] = row
    s4[...] = jnp.zeros_like(s4)
    s5[...] = jnp.zeros_like(s5)

    pl.semaphore_wait(barrier, len(peers))

    def hop(way, dist, half):
        side = 0 if way > 0 else 1
        part = pl.ds(half * 64, 64)
        src = tok.at[part] if dist == 1 else ring.at[2 * (dist - 2) + side, part]
        slot = 6 if dist == 4 else 2 * (dist - 1) + side
        return remote(
            src, ring.at[slot, part], ring_ss.at[side, dist - 1, half], ring_rs.at[side, dist - 1, half],
            y_peer(way),
        )

    def arrive(dist, half):
        for way in (1, -1):
            if dist < 4 or (half == 0) == (way > 0):
                hop(way, dist, half).wait_recv()
                if dist < 3 or (dist == 3 and (half == 0) == (way > 0)):
                    send(hop(way, dist + 1, half))

    for half in (0, 1):
        for way in (1, -1):
            send(hop(way, 1, half))

    away = pl.ds((1 - zl) * NY, NY)
    here = pl.ds(zl * NY, NY)
    swap_q = send(remote(q.at[away], qp, z_ss.at[0], z_rs.at[0], z_peer))
    swap_do = send(remote(do.at[away], dop, z_ss.at[1], z_rs.at[1], z_peer))
    swap_w = send(remote(w.at[c, :, pl.ds(0, HD)], w.at[c, :, pl.ds(HD, HD)], w_ss.at[0], w_rs.at[0], z_peer))
    c1 = [send(remote(prow.at[zl, y], prow.at[zl, y], c1_ss.at[k], c1_rs.at[k], y_peer(k))) for k in range(1, NY)]

    def attend(count, sources, load, first):
        tokens = load()
        keys2 = nn(tokens, w[0]).astype(BF16)
        values2 = nn(tokens, w[1]).astype(BF16)
        spots = lax.broadcasted_iota(jnp.int32, (32, 128), 0)
        grads_k, grads_v = [], []
        for i in range(count):
            src = sources[i]
            b = zl * NY + src
            keep = spots < length[b]
            both_k, both_v = [], []
            for h in range(2):
                query = q[b] if h == 0 else qp[src]
                cot = do[b] if h == 0 else dop[src]
                part = slice(i * 128, (i + 1) * 128)
                cols = slice(h * HD, (h + 1) * HD)
                key, value = keys2[part, cols], values2[part, cols]
                scores = nt(query, key) * ROOT
                top = jnp.max(scores, axis=1, keepdims=True)
                e = jnp.exp(scores - top)
                probs = e / jnp.sum(e, axis=1, keepdims=True)
                probs_b = probs.astype(BF16)
                out = jnp.where(keep, nn(probs_b, value), 0.0).astype(BF16)
                masked = jnp.where(keep, cot.astype(F32), 0.0).astype(BF16)
                both_v.append(tn(probs_b, masked).astype(BF16))
                grad_probs = nt(masked, value)
                dots = jnp.sum(probs * grad_probs, axis=1, keepdims=True)
                grad_scores = (probs * (grad_probs - dots) * ROOT).astype(BF16)
                grad_q = nn(grad_scores, key).astype(BF16)
                both_k.append(tn(grad_scores, query).astype(BF16))
                if h == 0:
                    att[b] = out
                    gq[b] = grad_q
                else:
                    att_s[src] = out
                    gq_s[src] = grad_q
            grads_k.append(jnp.concatenate(both_k, axis=1))
            grads_v.append(jnp.concatenate(both_v, axis=1))
        grad_k = grads_k[0] if count == 1 else jnp.concatenate(grads_k, axis=0)
        grad_v = grads_v[0] if count == 1 else jnp.concatenate(grads_v, axis=0)
        for n, grad in ((0, grad_k), (1, grad_v)):
            term = tn(tokens, grad)
            if first:
                acc[n] = term
            else:
                acc[n] += term

    def pair(dist):
        lo = 2 * (dist - 1)
        attend(2, [y_at(-dist), y_at(dist)], lambda: ring[lo : lo + 2].reshape(256, DI), False)

    arrive(1, 0)
    for copy in c1:
        copy.wait_recv()
    c2 = send(remote(prow.at[zl], prow.at[zl], c2_ss, c2_rs, z_peer))

    arrive(1, 1)
    swap_w.wait_recv()
    share_w = send(remote(w.at[c, :, pl.ds(HD, HD)], w.at[c, :, pl.ds(HD, HD)], w_ss.at[1], w_rs.at[1], c_peer))
    remote(prow.at[zl], prow.at[1 - zl], c2_ss, c2_rs, z_peer).wait_recv()
    part = jnp.zeros((16, HD), F32)
    for i in range(DI // 128):
        piece = prow[:, :, i, :].reshape(16, 128).astype(BF16)
        part += nn(piece, wp[i * 128 : (i + 1) * 128, :])
    mine = jnp.concatenate([part.astype(BF16), txt[...]], axis=0)
    gbuf[x, zh, c] = mine
    c3a = send(remote(gbuf.at[x, zh, c], gbuf.at[x, zh, c], c3_ss.at[0], c3_rs.at[0], c_peer))
    swap_q.wait_recv()
    swap_do.wait_recv()
    c3a.wait_recv()
    c3b = [
        send(remote(gbuf.at[x, zh], gbuf.at[x, zh], c3_ss.at[k], c3_rs.at[k], x_peer(k))) for k in range(1, NX)
    ]
    share_w.wait_recv()

    attend(1, [y], lambda: tok[...], True)
    arrive(2, 0)
    for copy in c3b:
        copy.wait_recv()
    c3c = [
        send(remote(gbuf.at[:, zh], gbuf.at[:, zh], c3_ss.at[3 + k], c3_rs.at[3 + k], h_peer(k)))
        for k in range(1, NZH)
    ]
    arrive(2, 1)
    pair(1)
    arrive(3, 0)
    for copy in c3c:
        copy.wait_recv()
    every = gbuf[...].reshape(512 // 16, 32, HD)
    all_img = every[:, :16].reshape(512, HD)
    all_txt = every[:, 16:].reshape(512, HD)
    own = gbuf[x, zh, c]
    dots_img = nt(own[:16], all_txt)
    dots_txt = nt(own[16:], all_img)
    ones = jnp.ones((8, HD), F32)

    def squares(rows_):
        wide = rows_.astype(F32)
        return lax.dot_general(
            ones, wide * wide, (((1,), (1,)), ((), ())),
            preferred_element_type=F32, precision=lax.Precision.HIGHEST,
        )

    sq_img, sq_txt = squares(all_img), squares(all_txt)
    for k in range(NY):
        pk[k, 0:2] = dots_img[2 * k : 2 * k + 2]
        pk[k, 2:4] = dots_txt[2 * k : 2 * k + 2]
        pk[k, 4:6] = sq_img[4:6]
        pk[k, 6:8] = sq_txt[6:8]
    c4 = [
        send(remote(pk.at[y_at(k)], rk.at[k], c4_ss.at[k], c4_rs.at[k], y_peer(k))) for k in range(1, NY)
    ]
    pair(2)
    arrive(3, 1)
    total = pk[y]
    for k in range(1, NY):
        c4[k - 1].wait_recv()
        total += rk[k]
    zs[...] = total
    c5 = send(remote(zs, zr, c5_ss, c5_rs, z_peer))
    pair(3)
    c5.wait_recv()
    total = zs[...] + zr[...]
    spot = lax.broadcasted_iota(jnp.int32, (2, 512), 1)
    index = d * 16 + 2 * y + lax.broadcasted_iota(jnp.int32, (2, 512), 0)
    hit = spot == index
    sq_i, sq_t = total[4:5], total[6:7]

    def side(dots, sq_rows, sq_cols):
        sq_row = jnp.sum(jnp.where(hit, sq_rows, 0.0), axis=1, keepdims=True)
        logits = temp[0] * dots * lax.rsqrt(sq_row + 1e-6) * lax.rsqrt(sq_cols + 1e-6)
        top = jnp.max(logits, axis=1, keepdims=True)
        lse = top + jnp.log(jnp.sum(jnp.exp(logits - top), axis=1, keepdims=True))
        return lse - jnp.sum(jnp.where(hit, logits, 0.0), axis=1, keepdims=True)

    img_side = side(total[0:2], sq_i, sq_t)
    txt_side = side(total[2:4], sq_t, sq_i)
    lane = lax.broadcasted_iota(jnp.int32, (8, 128), 1)
    line = lax.broadcasted_iota(jnp.int32, (8, 128), 0)
    tile = jnp.zeros((8, 128), F32)
    for r in range(2):
        here_lane = lane == 2 * y + r
        tile = jnp.where(here_lane & (line == 0), img_side[r : r + 1], tile)
        tile = jnp.where(here_lane & (line == 1), txt_side[r : r + 1], tile)
    cs[...] = tile
    c6 = [send(remote(cs, cr.at[k], c6_ss.at[k], c6_rs.at[k], y_peer(k))) for k in range(1, NY)]

    arrive(4, 0)
    arrive(4, 1)
    attend(1, [y_at(4)], lambda: ring[6], False)

    back = [
        send(remote(att_s, att_r, z_ss.at[2], z_rs.at[2], z_peer)),
        send(remote(gq_s, gq_r, z_ss.at[3], z_rs.at[3], z_peer)),
    ]

    XR, HR, CR = DI // NX, DI // (NX * NZH), DI // (NX * NZH * NC)

    def block(k):
        return pl.ds(pl.multiple_of(x_at(k) * XR, 32), XR)

    order = (1, 2, 3, 0)
    t1 = {}
    for k in order:
        s1[block(k), :] = acc[1 - c, block(k), :].astype(BF16)
        t1[k] = send(remote(s1.at[block(k)], r1.at[block(k)], t1_ss.at[k], t1_rs.at[k], c_peer))
    t2 = {}
    for k in order:
        t1[k].wait_recv()
        both = acc[c, block(k), :] + r1[block(k), :].astype(F32)
        own2[k] = both[:, :HD]
        s2[k] = both[:, HD:].astype(BF16)
        t2[k] = send(remote(s2.at[k], r2.at[k], t2_ss.at[k], t2_rs.at[k], z_peer))
    t3c = {}
    for k in order[:3]:
        t2[k].wait_recv()
        s3[k] = (own2[k] + r2[k].astype(F32)).astype(BF16)
        t3c[k] = send(remote(s3.at[k], r3.at[k], t3_ss.at[k], t3_rs.at[k], x_peer(k)))
    t2[0].wait_recv()
    block_sum = own2[0] + r2[0].astype(F32)
    for k in order[:3]:
        t3c[k].wait_recv()
        block_sum += r3[k].astype(F32)
    t3[...] = block_sum
    t4 = []
    for k in range(1, NZH):
        s4[k, 0:HR] = t3[pl.ds(pl.multiple_of(h_at(k) * HR, 8), HR), :].astype(BF16)
        t4.append(send(remote(s4.at[k], r4.at[k], t4_ss.at[k], t4_rs.at[k], h_peer(k))))
    piece = t3[pl.ds(pl.multiple_of(zh * HR, 8), HR), :]
    for k in range(1, NZH):
        t4[k - 1].wait_recv()
        piece += r4[k, 0:HR].astype(F32)
    low, high = piece[:CR], piece[CR:]
    s5[0:CR] = jnp.where(c == 0, high, low)
    t5 = send(remote(s5, r5, t5_ss, t5_rs, c_peer))
    kept = jnp.where(c == 0, low, high)

    for copy in back:
        copy.wait_recv()
    att[away] = att_r[...]
    gq[away] = gq_r[...]
    answer = cs[...]
    for k in range(1, NY):
        c6[k - 1].wait_recv()
        answer += cr[k]
    con[...] = answer[0:2, 0:16]
    t5.wait_recv()
    got = r5[0:CR]
    dwk[...] = jnp.where(c == 0, kept, got)
    dwv[...] = jnp.where(c == 0, got, kept)
    for copy in sent:
        copy.wait_send()


def body(img_tokens, w_key, w_value, queries, lengths, d_out, img_pooled, w_proj, txt_embed, inv_temp):
    vmem = pl.BlockSpec(memory_space=pltpu.VMEM)
    smem = pl.BlockSpec(memory_space=pltpu.SMEM)
    dma = pltpu.SemaphoreType.DMA
    V = pltpu.VMEM
    return pl.pallas_call(
        kernel,
        out_shape=(
            jax.ShapeDtypeStruct((16, 32, HD), BF16),
            jax.ShapeDtypeStruct((16, 32, HD), BF16),
            jax.ShapeDtypeStruct((44, HD), F32),
            jax.ShapeDtypeStruct((44, HD), F32),
            jax.ShapeDtypeStruct((2, 16), F32),
        ),
        in_specs=[vmem, vmem, vmem, vmem, smem, vmem, vmem, vmem, vmem, smem],
        out_specs=(vmem,) * 5,
        scratch_shapes=[
            V((7, 128, DI), BF16),
            V((2, DI, 256), BF16),
            V((8, 32, HD), BF16),
            V((8, 32, HD), BF16),
            V((8, 32, HD), BF16),
            V((8, 32, HD), BF16),
            V((8, 32, HD), BF16),
            V((8, 32, HD), BF16),
            V((2, DI, 256), F32),
            V((DI, 256), BF16),
            V((DI, 256), BF16),
            V((4, 352, HD), F32),
            V((4, 352, HD), BF16),
            V((4, 352, HD), BF16),
            V((4, 352, HD), BF16),
            V((4, 352, HD), BF16),
            V((352, HD), F32),
            V((4, 96, HD), BF16),
            V((4, 96, HD), BF16),
            V((48, HD), F32),
            V((48, HD), F32),
            V((2, 8, 16, 128), F32),
            V((4, 4, 2, 32, HD), BF16),
            V((8, 8, 512), F32),
            V((8, 8, 512), F32),
            V((8, 512), F32),
            V((8, 512), F32),
            V((8, 128), F32),
            V((8, 8, 128), F32),
            dma((2, 4, 2)), dma((2, 4, 2)),
            dma((4,)), dma((4,)),
            dma((2,)), dma((2,)),
            dma((8,)), dma((8,)),
            dma, dma,
            dma((8,)), dma((8,)),
            dma((8,)), dma((8,)),
            dma, dma,
            dma((8,)), dma((8,)),
            dma((4,)), dma((4,)),
            dma((4,)), dma((4,)),
            dma((4,)), dma((4,)),
            dma((4,)), dma((4,)),
            dma, dma,
        ],
        compiler_params=pltpu.CompilerParams(
            collective_id=0, has_side_effects=True, vmem_limit_bytes=48 * 1024 * 1024
        ),
        cost_estimate=pl.CostEstimate(flops=6_200_000_000, bytes_accessed=4_000_000, transcendentals=100_000),
    )(
        img_tokens.reshape(128, DI), w_key, w_value, queries, lengths, d_out, img_pooled, w_proj, txt_embed, inv_temp
    )


def solution(mesh):
    placed = (
        P(("dp", "mp"), None, None),
        P(None, "mp"),
        P(None, "mp"),
        P("dp", None, "mp"),
        P("dp"),
        P("dp", None, "mp"),
        P(("dp", "mp"), None),
        P(None, "mp"),
        P("dp", "mp"),
        P(),
    )
    return jax.shard_map(
        body,
        mesh=mesh,
        in_specs=placed,
        out_specs=(
            P("dp", None, "mp"),
            P("dp", None, "mp"),
            P("dp", "mp"),
            P("dp", "mp"),
            P(None, "dp"),
        ),
        check_vma=False,
    )
```

time: 596 us -> 94.2 us (0.16)
  waiting for transfers between devices: 459 us -> 0 us
  blocking collectives: 81.9 us -> 0 us
  Pallas kernels: 0 us -> 81.7 us
  matrix products: 24.5 us -> 0 us
  between operations: 15.2 us -> 1.31 us
  other arithmetic: 8.74 us -> 0 us
    unnamed x5 -> x0, waiting for transfers between devices: 287 us -> none
    all_gather x3 -> x0, waiting for transfers between devices: 172 us -> none  [the longest x1 69.8 us: body(): all_tokens = lax.all_gather(img_tokens, 'mp', axis=0, tiled=True)]
    all_gather x3 -> x0, blocking collectives: 81.9 us -> none  [the longest x1 29.2 us: body(): pooled_group = lax.all_gather(img_pooled, 'mp', axis=0, tiled=True)]
    pallas_call x0 -> x1, Pallas kernels: none -> 81.7 us  [body(): pl.pallas_call(kernel, out_shape=(jax.ShapeDtypeStruct((16, 32, HD), BF16...]
    dot_general x11 -> x0, matrix products: 24.5 us -> none  [the longest x1 5.73 us: weight_terms(): jnp.einsum('rc,re->ce', flat_tokens, flat_grads, preferred_element_type=j...]
    unnamed x17 -> x23, local copies, waits for them, and re-layouts: 3.04 us -> 10.9 us
  transfers between devices with their start and end apart: 4 -> 0, of which waited for: 4 -> 0; matrix products, arithmetic and copies ran while one was open for 3% -> 0% of each run, Pallas kernels for 0% -> 0%
where the time goes in v1:
time: 94.2 us; the launch traced here: 93.8 us
  Pallas kernels  81.7 us (87%)
  local copies, waits for them, and re-layouts  10.9 us (12%)
  between operations  1.31 us (1%)
    pallas_call x1, Pallas kernels, body(): pl.pallas_call(kernel, out_shape=(jax.ShapeDtypeStruct((16, 32, HD), BF16...  81.7 us
    unnamed x23, local copies, waits for them, and re-layouts  10.9 us

profile of v1, /device:TPU:1, one launch (start us, length us, event | category | flops | bytes accessed | tf_op | source)
XLA Modules:
  0.0 93.8 jit_solution(4244315552925925799)
XLA Ops:
  1.3 0.0 copy-start.8
  1.3 0.6 copy-done.8
  1.9 0.0 copy-start
  1.9 1.0 %copy-done = bf16[1,128,1408]{2,1,0:T(8,128)(2,1)S(1)} copy-done((bf16[1,128,1408]{2,1,0:T(8,128)(2,1)S(1)}, bf16[1,128,1408]{2,1,0:T(8,128)(2,1)}, u32[]{:S(2)}) %copy-start) | copy-done | bytes 360472
  2.9 0.0 copy-start.1
  2.9 1.0 %copy-done.1 = bf16[1408,128]{1,0:T(8,128)(2,1)S(1)} copy-done((bf16[1408,128]{1,0:T(8,128)(2,1)S(1)}, bf16[1408,128]{1,0:T(8,128)(2,1)}, u32[]{:S(2)}) %copy-start.1) | copy-done | bytes 360472
  3.9 0.0 copy-start.2
  3.9 1.0 %copy-done.2 = bf16[1408,128]{1,0:T(8,128)(2,1)S(1)} copy-done((bf16[1408,128]{1,0:T(8,128)(2,1)S(1)}, bf16[1408,128]{1,0:T(8,128)(2,1)}, u32[]{:S(2)}) %copy-start.2) | copy-done | bytes 360472
  4.9 0.0 copy-start.3
  4.9 1.0 %copy-done.3 = bf16[1408,128]{1,0:T(8,128)(2,1)S(1)} copy-done((bf16[1408,128]{1,0:T(8,128)(2,1)S(1)}, bf16[1408,128]{1,0:T(8,128)(2,1)}, u32[]{:S(2)}) %copy-start.3) | copy-done | bytes 360472
  5.9 0.0 copy-start.4
  5.9 0.9 copy-done.4
  6.8 0.0 copy-start.5
  6.8 0.9 copy-done.5
  7.7 0.0 copy-start.6
  7.7 0.7 copy-done.6
  8.4 0.0 copy-start.7
  8.4 0.7 copy-done.7
  9.1 81.7 %shard_map.137 = (bf16[16,32,128]{2,1,0:T(8,128)(2,1)S(1)}, bf16[16,32,128]{2,1,0:T(8,128)(2,1)S(1)}, f32[44,128]{1,0:T(8,128)S(1)}, f32[44,128]{1,0:T(8,128)S(1)}, f32[2,16]{1,0:T(2,128)S(1)}) custom-call(bf16[128,1408]{1,0:T(8,128)(2,1)S(1)} %bitcast.1, bf16[1408,128]{1,0:T(8,128)(2,1)S(1)} %copy-done.1, bf16[1408,128]{1,0:T(8,128)(2,1)S(1)} %copy-done.2, ...), custom_call_target="tpu_custom_call" | custom-call | flops 6200000000 | bytes 4000000 | tf_op jit(solution)/shard_map/pallas_call | solution.py:345
  90.8 0.7 copy.21
  91.4 0.7 copy.22
  92.1 0.6 copy.23
  92.7 0.6 copy.24
  93.3 0.6 copy.25
Async XLA Ops:
  1.3 0.7 copy-start.8
  1.9 1.0 %copy-start = (bf16[1,128,1408]{2,1,0:T(8,128)(2,1)S(1)}, bf16[1,128,1408]{2,1,0:T(8,128)(2,1)}, u32[]{:S(2)}) copy-start(bf16[1,128,1408]{2,1,0:T(8,128)(2,1)} %param.10) | copy-start | bytes 1081348
  2.9 1.0 %copy-start.1 = (bf16[1408,128]{1,0:T(8,128)(2,1)S(1)}, bf16[1408,128]{1,0:T(8,128)(2,1)}, u32[]{:S(2)}) copy-start(bf16[1408,128]{1,0:T(8,128)(2,1)} %wk.1) | copy-start | bytes 1081348
  3.9 1.0 %copy-start.2 = (bf16[1408,128]{1,0:T(8,128)(2,1)S(1)}, bf16[1408,128]{1,0:T(8,128)(2,1)}, u32[]{:S(2)}) copy-start(bf16[1408,128]{1,0:T(8,128)(2,1)} %wv.1) | copy-start | bytes 1081348
  4.9 1.0 %copy-start.3 = (bf16[1408,128]{1,0:T(8,128)(2,1)S(1)}, bf16[1408,128]{1,0:T(8,128)(2,1)}, u32[]{:S(2)}) copy-start(bf16[1408,128]{1,0:T(8,128)(2,1)} %wp.1) | copy-start | bytes 1081348
  5.9 0.9 copy-start.4
  6.8 0.9 copy-start.5
  7.7 0.7 copy-start.6
  8.4 0.7 copy-start.7

commit v2 on v1

--- a/solution.py
+++ b/solution.py
@@ -29,11 +29,12 @@
 
 
 def kernel(
-    tok, wk, wv, q, length, do, pooled, wp, txt, temp,
+    tok_in, wk, wv, q_in, length_in, do_in, pooled_in, wp_in, txt_in, temp,
     att, gq, dwk, dwv, con,
+    tok, q, length, do, pooled, wp, txt, in_sem,
     ring, w, qp, dop, att_s, gq_s, att_r, gq_r, acc,
-    s1, r1, own2, s2, r2, s3, r3, t3, s4, r4, s5, r5,
-    prow, gbuf, pk, rk, zs, zr, cs, cr,
+    s1, r1, own2, s2, r2, s3, r3, own_w, s3w, r3w, t3, s4, r4, s5, r5,
+    prow, gbuf, pk, pz, pk2, rk, cs, cr,
     ring_ss, ring_rs, z_ss, z_rs, w_ss, w_rs, c1_ss, c1_rs, c2_ss, c2_rs, c3_ss, c3_rs,
     c4_ss, c4_rs, c5_ss, c5_rs, c6_ss, c6_rs, t1_ss, t1_rs, t2_ss, t2_rs, t3_ss, t3_rs,
     t4_ss, t4_rs, t5_ss, t5_rs,
@@ -76,14 +77,26 @@
         sent.append(copy)
         return copy
 
+    loads = [
+        pltpu.make_async_copy(src, dst, in_sem.at[i])
+        for i, (src, dst) in enumerate(
+            (
+                (wk, w.at[0, :, pl.ds(0, HD)]), (wv, w.at[1, :, pl.ds(0, HD)]), (pooled_in, pooled),
+                (tok_in, tok), (q_in, q), (do_in, do), (wp_in, wp), (txt_in, txt), (length_in, length),
+            )
+        )
+    ]
+    for copy in loads:
+        copy.start()
+
     barrier = pltpu.get_barrier_semaphore()
     peers = [y_peer(k) for k in range(1, NY)] + [z_peer, c_peer]
     peers += [x_peer(k) for k in range(1, NX)] + [h_peer(k) for k in range(1, NZH)]
     for peer in peers:
         pl.semaphore_signal(barrier, inc=1, device_id=peer, device_id_type=MESH)
 
-    w[0, :, 0:HD] = wk[...]
-    w[1, :, 0:HD] = wv[...]
+    for copy in loads:
+        copy.wait()
     row = jnp.zeros((16, 128), F32)
     rows = lax.broadcasted_iota(jnp.int32, (16, 128), 0)
     for i in range(DI // 128):
@@ -98,7 +111,7 @@
     def hop(way, dist, half):
         side = 0 if way > 0 else 1
         part = pl.ds(half * 64, 64)
-        src = tok.at[part] if dist == 1 else ring.at[2 * (dist - 2) + side, part]
+        src = tok_in.at[part] if dist == 1 else ring.at[2 * (dist - 2) + side, part]
         slot = 6 if dist == 4 else 2 * (dist - 1) + side
         return remote(
             src, ring.at[slot, part], ring_ss.at[side, dist - 1, half], ring_rs.at[side, dist - 1, half],
@@ -112,19 +125,16 @@
                 if dist < 3 or (dist == 3 and (half == 0) == (way > 0)):
                     send(hop(way, dist + 1, half))
 
+    c1 = [send(remote(prow.at[zl, y], prow.at[zl, y], c1_ss.at[k], c1_rs.at[k], y_peer(k))) for k in range(1, NY)]
     for half in (0, 1):
         for way in (1, -1):
             send(hop(way, 1, half))
-
     away = pl.ds((1 - zl) * NY, NY)
-    here = pl.ds(zl * NY, NY)
-    swap_q = send(remote(q.at[away], qp, z_ss.at[0], z_rs.at[0], z_peer))
-    swap_do = send(remote(do.at[away], dop, z_ss.at[1], z_rs.at[1], z_peer))
     swap_w = send(remote(w.at[c, :, pl.ds(0, HD)], w.at[c, :, pl.ds(HD, HD)], w_ss.at[0], w_rs.at[0], z_peer))
-    c1 = [send(remote(prow.at[zl, y], prow.at[zl, y], c1_ss.at[k], c1_rs.at[k], y_peer(k))) for k in range(1, NY)]
-
-    def attend(count, sources, load, first):
-        tokens = load()
+    swap_q = send(remote(q_in.at[away], qp, z_ss.at[0], z_rs.at[0], z_peer))
+    swap_do = send(remote(do_in.at[away], dop, z_ss.at[1], z_rs.at[1], z_peer))
+
+    def attend(count, sources, tokens):
         keys2 = nn(tokens, w[0]).astype(BF16)
         values2 = nn(tokens, w[1]).astype(BF16)
         spots = lax.broadcasted_iota(jnp.int32, (32, 128), 0)
@@ -163,52 +173,56 @@
             grads_v.append(jnp.concatenate(both_v, axis=1))
         grad_k = grads_k[0] if count == 1 else jnp.concatenate(grads_k, axis=0)
         grad_v = grads_v[0] if count == 1 else jnp.concatenate(grads_v, axis=0)
-        for n, grad in ((0, grad_k), (1, grad_v)):
-            term = tn(tokens, grad)
-            if first:
-                acc[n] = term
-            else:
-                acc[n] += term
+        return grad_k, grad_v
 
     def pair(dist):
         lo = 2 * (dist - 1)
-        attend(2, [y_at(-dist), y_at(dist)], lambda: ring[lo : lo + 2].reshape(256, DI), False)
+        tokens = ring[lo : lo + 2].reshape(256, DI)
+        grad_k, grad_v = attend(2, [y_at(-dist), y_at(dist)], tokens)
+        acc[0] += tn(tokens, grad_k)
+        acc[1] += tn(tokens, grad_v)
 
     arrive(1, 0)
+    arrive(1, 1)
     for copy in c1:
         copy.wait_recv()
     c2 = send(remote(prow.at[zl], prow.at[zl], c2_ss, c2_rs, z_peer))
-
-    arrive(1, 1)
     swap_w.wait_recv()
     share_w = send(remote(w.at[c, :, pl.ds(HD, HD)], w.at[c, :, pl.ds(HD, HD)], w_ss.at[1], w_rs.at[1], c_peer))
-    remote(prow.at[zl], prow.at[1 - zl], c2_ss, c2_rs, z_peer).wait_recv()
+
+    arrive(2, 0)
+    swap_q.wait_recv()
+    swap_do.wait_recv()
+    share_w.wait_recv()
+    grad_k, grad_v = attend(1, [y], tok[...])
+    acc[0] = tn(tok[...], grad_k)
+    acc[1] = tn(tok[...], grad_v)
+    c2.wait_recv()
     part = jnp.zeros((16, HD), F32)
     for i in range(DI // 128):
         piece = prow[:, :, i, :].reshape(16, 128).astype(BF16)
         part += nn(piece, wp[i * 128 : (i + 1) * 128, :])
-    mine = jnp.concatenate([part.astype(BF16), txt[...]], axis=0)
-    gbuf[x, zh, c] = mine
+    gbuf[x, zh, c] = jnp.concatenate([part.astype(BF16), txt[...]], axis=0)
     c3a = send(remote(gbuf.at[x, zh, c], gbuf.at[x, zh, c], c3_ss.at[0], c3_rs.at[0], c_peer))
-    swap_q.wait_recv()
-    swap_do.wait_recv()
+
+    arrive(2, 1)
     c3a.wait_recv()
     c3b = [
         send(remote(gbuf.at[x, zh], gbuf.at[x, zh], c3_ss.at[k], c3_rs.at[k], x_peer(k))) for k in range(1, NX)
     ]
-    share_w.wait_recv()
-
-    attend(1, [y], lambda: tok[...], True)
-    arrive(2, 0)
+    pair(1)
+
+    arrive(3, 0)
     for copy in c3b:
         copy.wait_recv()
     c3c = [
         send(remote(gbuf.at[:, zh], gbuf.at[:, zh], c3_ss.at[3 + k], c3_rs.at[3 + k], h_peer(k)))
         for k in range(1, NZH)
     ]
-    arrive(2, 1)
-    pair(1)
-    arrive(3, 0)
+    pair(2)
+
+    arrive(3, 1)
+    pair(3)
     for copy in c3c:
         copy.wait_recv()
     every = gbuf[...].reshape(512 // 16, 32, HD)
@@ -232,20 +246,67 @@
         pk[k, 2:4] = dots_txt[2 * k : 2 * k + 2]
         pk[k, 4:6] = sq_img[4:6]
         pk[k, 6:8] = sq_txt[6:8]
-    c4 = [
-        send(remote(pk.at[y_at(k)], rk.at[k], c4_ss.at[k], c4_rs.at[k], y_peer(k))) for k in range(1, NY)
+    c4 = send(remote(pk, pz, c4_ss, c4_rs, z_peer))
+
+    arrive(4, 0)
+    arrive(4, 1)
+    tokens = ring[6]
+    grad_k, grad_v = attend(1, [y_at(4)], tokens)
+
+    XR, HR, CR = DI // NX, DI // (NX * NZH), DI // (NX * NZH * NC)
+    theirs = jnp.where(c == 0, grad_v.astype(F32), grad_k.astype(F32)).astype(BF16)
+    ours = jnp.where(c == 0, grad_k.astype(F32), grad_v.astype(F32)).astype(BF16)
+    t1 = []
+    for i, (lo, hi) in enumerate(((0, 512), (512, 1024), (1024, DI))):
+        s1[lo:hi] = (acc[1 - c, lo:hi] + tn(tokens[:, lo:hi], theirs)).astype(BF16)
+        t1.append(send(remote(s1.at[lo:hi], r1.at[lo:hi], t1_ss.at[i], t1_rs.at[i], c_peer)))
+    acc[c] += tn(tokens, ours)
+    back = [
+        send(remote(att_s, att_r, z_ss.at[2], z_rs.at[2], z_peer)),
+        send(remote(gq_s, gq_r, z_ss.at[3], z_rs.at[3], z_peer)),
     ]
-    pair(2)
-    arrive(3, 1)
-    total = pk[y]
+    c4.wait_recv()
+    for k in range(NY):
+        pk2[k] = pk[k] + pz[k]
+    c5 = [
+        send(remote(pk2.at[y_at(k)], rk.at[k], c5_ss.at[k], c5_rs.at[k], y_peer(k))) for k in range(1, NY)
+    ]
+
+    def block(k):
+        return pl.ds(pl.multiple_of(x_at(k) * XR, 32), XR)
+
+    def over_z(k):
+        return remote(s2.at[k], r2.at[k], t2_ss.at[k], t2_rs.at[k], z_peer)
+
+    def over_x(k):
+        return remote(s3.at[k], r3.at[k], t3_ss.at[k], t3_rs.at[k], x_peer(k))
+
+    def over_x2(k):
+        return remote(s3w.at[k], r3w.at[k], t3_ss.at[k], t3_rs.at[k], x_peer(k))
+
+    order = (2, 1, 3)
+    for copy in t1:
+        copy.wait_recv()
+
+    @pl.when(c == 0)
+    def _():
+        for k in order + (0,):
+            both = acc[0, block(k), :] + r1[block(k), :].astype(F32)
+            own2[k] = both[:, :HD]
+            s2[k] = both[:, HD:].astype(BF16)
+            over_z(k).start()
+
+    @pl.when(c == 1)
+    def _():
+        for k in order:
+            s3w[k] = (acc[1, block(k), :] + r1[block(k), :].astype(F32)).astype(BF16)
+            over_x2(k).start()
+        own_w[...] = acc[1, block(0), :] + r1[block(0), :].astype(F32)
+
+    total = pk2[y]
     for k in range(1, NY):
-        c4[k - 1].wait_recv()
+        c5[k - 1].wait_recv()
         total += rk[k]
-    zs[...] = total
-    c5 = send(remote(zs, zr, c5_ss, c5_rs, z_peer))
-    pair(3)
-    c5.wait_recv()
-    total = zs[...] + zr[...]
     spot = lax.broadcasted_iota(jnp.int32, (2, 512), 1)
     index = d * 16 + 2 * y + lax.broadcasted_iota(jnp.int32, (2, 512), 0)
     hit = spot == index
@@ -270,56 +331,36 @@
     cs[...] = tile
     c6 = [send(remote(cs, cr.at[k], c6_ss.at[k], c6_rs.at[k], y_peer(k))) for k in range(1, NY)]
 
-    arrive(4, 0)
-    arrive(4, 1)
-    attend(1, [y_at(4)], lambda: ring[6], False)
-
-    back = [
-        send(remote(att_s, att_r, z_ss.at[2], z_rs.at[2], z_peer)),
-        send(remote(gq_s, gq_r, z_ss.at[3], z_rs.at[3], z_peer)),
-    ]
-
-    XR, HR, CR = DI // NX, DI // (NX * NZH), DI // (NX * NZH * NC)
-
-    def block(k):
-        return pl.ds(pl.multiple_of(x_at(k) * XR, 32), XR)
-
-    order = (1, 2, 3, 0)
-    t1 = {}
-    for k in order:
-        s1[block(k), :] = acc[1 - c, block(k), :].astype(BF16)
-        t1[k] = send(remote(s1.at[block(k)], r1.at[block(k)], t1_ss.at[k], t1_rs.at[k], c_peer))
-    t2 = {}
-    for k in order:
-        t1[k].wait_recv()
-        both = acc[c, block(k), :] + r1[block(k), :].astype(F32)
-        own2[k] = both[:, :HD]
-        s2[k] = both[:, HD:].astype(BF16)
-        t2[k] = send(remote(s2.at[k], r2.at[k], t2_ss.at[k], t2_rs.at[k], z_peer))
-    t3c = {}
-    for k in order[:3]:
-        t2[k].wait_recv()
-        s3[k] = (own2[k] + r2[k].astype(F32)).astype(BF16)
-        t3c[k] = send(remote(s3.at[k], r3.at[k], t3_ss.at[k], t3_rs.at[k], x_peer(k)))
-    t2[0].wait_recv()
-    block_sum = own2[0] + r2[0].astype(F32)
-    for k in order[:3]:
-        t3c[k].wait_recv()
-        block_sum += r3[k].astype(F32)
-    t3[...] = block_sum
+    @pl.when(c == 0)
+    def _():
+        for k in order:
+            over_z(k).wait_recv()
+            s3[k] = (own2[k] + r2[k].astype(F32)).astype(BF16)
+            over_x(k).start()
+        over_z(0).wait_recv()
+        block_sum = own2[0] + r2[0].astype(F32)
+        for k in order:
+            over_x(k).wait_recv()
+            block_sum += r3[k].astype(F32)
+        t3[...] = block_sum
+
+    @pl.when(c == 1)
+    def _():
+        for k in order:
+            over_x2(k).wait_recv()
+        wide = own_w[...]
+        for k in order:
+            wide += r3w[k].astype(F32)
+        s2[0] = wide[:, HD:].astype(BF16)
+        over_z(0).start()
+        over_z(0).wait_recv()
+        t3[...] = wide[:, :HD] + r2[0].astype(F32)
+
     t4 = []
     for k in range(1, NZH):
         s4[k, 0:HR] = t3[pl.ds(pl.multiple_of(h_at(k) * HR, 8), HR), :].astype(BF16)
         t4.append(send(remote(s4.at[k], r4.at[k], t4_ss.at[k], t4_rs.at[k], h_peer(k))))
     piece = t3[pl.ds(pl.multiple_of(zh * HR, 8), HR), :]
-    for k in range(1, NZH):
-        t4[k - 1].wait_recv()
-        piece += r4[k, 0:HR].astype(F32)
-    low, high = piece[:CR], piece[CR:]
-    s5[0:CR] = jnp.where(c == 0, high, low)
-    t5 = send(remote(s5, r5, t5_ss, t5_rs, c_peer))
-    kept = jnp.where(c == 0, low, high)
-
     for copy in back:
         copy.wait_recv()
     att[away] = att_r[...]
@@ -329,17 +370,42 @@
         c6[k - 1].wait_recv()
         answer += cr[k]
     con[...] = answer[0:2, 0:16]
+    for k in range(1, NZH):
+        t4[k - 1].wait_recv()
+        piece += r4[k, 0:HR].astype(F32)
+    low, high = piece[:CR], piece[CR:]
+    s5[0:CR] = jnp.where(c == 0, high, low)
+    t5 = send(remote(s5, r5, t5_ss, t5_rs, c_peer))
+    kept = jnp.where(c == 0, low, high)
+
+    for copy in sent:
+        if copy is not t5:
+            copy.wait_send()
+
+    @pl.when(c == 0)
+    def _():
+        for k in order + (0,):
+            over_z(k).wait_send()
+        for k in order:
+            over_x(k).wait_send()
+
+    @pl.when(c == 1)
+    def _():
+        for k in order:
+            over_x2(k).wait_send()
+        over_z(0).wait_send()
+
     t5.wait_recv()
     got = r5[0:CR]
     dwk[...] = jnp.where(c == 0, kept, got)
     dwv[...] = jnp.where(c == 0, got, kept)
-    for copy in sent:
-        copy.wait_send()
+    t5.wait_send()
 
 
 def body(img_tokens, w_key, w_value, queries, lengths, d_out, img_pooled, w_proj, txt_embed, inv_temp):
     vmem = pl.BlockSpec(memory_space=pltpu.VMEM)
     smem = pl.BlockSpec(memory_space=pltpu.SMEM)
+    hbm = pl.BlockSpec(memory_space=pltpu.HBM)
     dma = pltpu.SemaphoreType.DMA
     V = pltpu.VMEM
     return pl.pallas_call(
@@ -351,9 +417,17 @@
             jax.ShapeDtypeStruct((44, HD), F32),
             jax.ShapeDtypeStruct((2, 16), F32),
         ),
-        in_specs=[vmem, vmem, vmem, vmem, smem, vmem, vmem, vmem, vmem, smem],
+        in_specs=[hbm] * 9 + [smem],
         out_specs=(vmem,) * 5,
         scratch_shapes=[
+            V((128, DI), BF16),
+            V((16, 32, HD), BF16),
+            pltpu.SMEM((16,), jnp.int32),
+            V((16, 32, HD), BF16),
+            V((1, DI), BF16),
+            V((DI, HD), BF16),
+            V((16, HD), BF16),
+            dma((9,)),
             V((7, 128, DI), BF16),
             V((2, DI, 256), BF16),
             V((8, 32, HD), BF16),
@@ -370,6 +444,9 @@
             V((4, 352, HD), BF16),
             V((4, 352, HD), BF16),
             V((4, 352, HD), BF16),
+            V((352, 256), F32),
+            V((4, 352, 256), BF16),
+            V((4, 352, 256), BF16),
             V((352, HD), F32),
             V((4, 96, HD), BF16),
             V((4, 96, HD), BF16),
@@ -379,8 +456,8 @@
             V((4, 4, 2, 32, HD), BF16),
             V((8, 8, 512), F32),
             V((8, 8, 512), F32),
-            V((8, 512), F32),
-            V((8, 512), F32),
+            V((8, 8, 512), F32),
+            V((8, 8, 512), F32),
             V((8, 128), F32),
             V((8, 8, 128), F32),
             dma((2, 4, 2)), dma((2, 4, 2)),
@@ -388,18 +465,18 @@
             dma((2,)), dma((2,)),
             dma((8,)), dma((8,)),
             dma, dma,
+            dma((7,)), dma((7,)),
+            dma, dma,
             dma((8,)), dma((8,)),
             dma((8,)), dma((8,)),
-            dma, dma,
-            dma((8,)), dma((8,)),
-            dma((4,)), dma((4,)),
+            dma((3,)), dma((3,)),
             dma((4,)), dma((4,)),
             dma((4,)), dma((4,)),
             dma((4,)), dma((4,)),
             dma, dma,
         ],
         compiler_params=pltpu.CompilerParams(
-            collective_id=0, has_side_effects=True, vmem_limit_bytes=48 * 1024 * 1024
+            collective_id=0, has_side_effects=True, vmem_limit_bytes=60 * 1024 * 1024
         ),
         cost_estimate=pl.CostEstimate(flops=6_200_000_000, bytes_accessed=4_000_000, transcendentals=100_000),
     )(

time: 94.2 us -> 76.8 us (0.82)
  Pallas kernels: 81.7 us -> 70.9 us
  local copies, waits for them, and re-layouts: 10.9 us -> 4.28 us
    pallas_call x1, Pallas kernels: 81.7 us -> 70.9 us  [body(): pl.pallas_call(kernel, out_shape=(jax.ShapeDtypeStruct((16, 32, HD), BF16...]
    unnamed x23 -> x13, local copies, waits for them, and re-layouts: 10.9 us -> 4.28 us
where the time goes in v2:
time: 76.8 us; the launch traced here: 76.5 us
  Pallas kernels  70.9 us (92%)
  local copies, waits for them, and re-layouts  4.28 us (6%)
  between operations  1.3 us (2%)
    pallas_call x1, Pallas kernels, body(): pl.pallas_call(kernel, out_shape=(jax.ShapeDtypeStruct((16, 32, HD), BF16...  70.9 us
    unnamed x13, local copies, waits for them, and re-layouts  4.28 us

profile of v2, /device:TPU:1, one launch (start us, length us, event | category | flops | bytes accessed | tf_op | source)
XLA Modules:
  0.0 76.5 jit_solution(2340940097984990679)
XLA Ops:
  1.3 70.9 %shard_map.137 = (bf16[16,32,128]{2,1,0:T(8,128)(2,1)}, bf16[16,32,128]{2,1,0:T(8,128)(2,1)}, f32[44,128]{1,0:T(8,128)}, f32[44,128]{1,0:T(8,128)}, f32[2,16]{1,0:T(2,128)}) custom-call(bf16[128,1408]{1,0:T(8,128)(2,1)} %bitcast.1, bf16[1408,128]{1,0:T(8,128)(2,1)} %wk.1, bf16[1408,128]{1,0:T(8,128)(2,1)} %wv.1, bf16[16,32,128]{2,1,0:T(8,128)(2,1)} %q_in.1, ...), custom_call_target="tpu_custom_call" | custom-call | flops 6200000000 | bytes 4000000 | tf_op jit(solution)/shard_map/pallas_call | solution.py:411
  72.2 0.0 copy-start
  72.2 1.6 %copy.21 = bf16[16,32,128]{2,1,0:T(8,128)(2,1)} copy(bf16[16,32,128]{2,1,0:T(8,128)(2,1)} %get-tuple-element.10) | data formatting | bytes 262144
  73.8 0.0 copy-done
  73.8 0.0 copy-start.2
  73.8 0.7 copy.22
  74.5 0.1 copy-done.2
  74.5 0.0 copy-start.1
  74.5 0.6 copy.23
  75.2 0.1 copy-done.1
  75.3 0.0 copy-start.3
  75.3 0.6 copy.24
  75.9 0.0 copy-done.3
  75.9 0.6 copy.25
Async XLA Ops:
  72.2 1.6 %copy-start = (bf16[16,32,128]{2,1,0:T(8,128)(2,1)S(1)}, bf16[16,32,128]{2,1,0:T(8,128)(2,1)}, u32[]{:S(2)}) copy-start(bf16[16,32,128]{2,1,0:T(8,128)(2,1)} %get-tuple-element.11) | copy-start | bytes 393220
  73.8 0.7 copy-start.2
  74.5 0.7 copy-start.1
  75.3 0.6 copy-start.3

commit v3 on v2

--- a/solution.py
+++ b/solution.py
@@ -30,15 +30,16 @@
 
 def kernel(
     tok_in, wk, wv, q_in, length_in, do_in, pooled_in, wp_in, txt_in, temp,
-    att, gq, dwk, dwv, con,
+    ag, dw, con,
     tok, q, length, do, pooled, wp, txt, in_sem,
-    ring, w, qp, dop, att_s, gq_s, att_r, gq_r, acc,
+    ring, w, qp, dop, out_s, out_r, acc, mine,
     s1, r1, own2, s2, r2, s3, r3, own_w, s3w, r3w, t3, s4, r4, s5, r5,
-    prow, gbuf, pk, pz, pk2, rk, cs, cr,
+    prow, pwide, gbuf, pk, pz, pk2, rk, cs, cr,
     ring_ss, ring_rs, z_ss, z_rs, w_ss, w_rs, c1_ss, c1_rs, c2_ss, c2_rs, c3_ss, c3_rs,
     c4_ss, c4_rs, c5_ss, c5_rs, c6_ss, c6_rs, t1_ss, t1_rs, t2_ss, t2_rs, t3_ss, t3_rs,
     t4_ss, t4_rs, t5_ss, t5_rs,
 ):
+    att, gq, dwk, dwv = ag.at[0], ag.at[1], dw.at[0], dw.at[1]
     d = lax.axis_index("dp")
     m = lax.axis_index("mp")
     x, zh, c = d // (NZH * NC), lax.rem(d // NC, NZH), lax.rem(d, NC)
@@ -81,7 +82,7 @@
         pltpu.make_async_copy(src, dst, in_sem.at[i])
         for i, (src, dst) in enumerate(
             (
-                (wk, w.at[0, :, pl.ds(0, HD)]), (wv, w.at[1, :, pl.ds(0, HD)]), (pooled_in, pooled),
+                (wk, w.at[0, :, pl.ds(0, HD)]), (wv, w.at[0, :, pl.ds(HD, HD)]), (pooled_in, pooled),
                 (tok_in, tok), (q_in, q), (do_in, do), (wp_in, wp), (txt_in, txt), (length_in, length),
             )
         )
@@ -102,7 +103,7 @@
     for i in range(DI // 128):
         piece = pooled[0:1, i * 128 : (i + 1) * 128].astype(F32)
         row = jnp.where(rows == i, piece, row)
-    prow[zl, y] = row
+    prow[zl, y] = row.astype(BF16)
     s4[...] = jnp.zeros_like(s4)
     s5[...] = jnp.zeros_like(s5)
 
@@ -125,92 +126,105 @@
                 if dist < 3 or (dist == 3 and (half == 0) == (way > 0)):
                     send(hop(way, dist + 1, half))
 
+    for way in (1, -1):
+        send(hop(way, 1, 0))
     c1 = [send(remote(prow.at[zl, y], prow.at[zl, y], c1_ss.at[k], c1_rs.at[k], y_peer(k))) for k in range(1, NY)]
-    for half in (0, 1):
-        for way in (1, -1):
-            send(hop(way, 1, half))
+    for way in (1, -1):
+        send(hop(way, 1, 1))
     away = pl.ds((1 - zl) * NY, NY)
-    swap_w = send(remote(w.at[c, :, pl.ds(0, HD)], w.at[c, :, pl.ds(HD, HD)], w_ss.at[0], w_rs.at[0], z_peer))
+    cols = pl.ds(pl.multiple_of(c * HD, HD), HD)
+    cols_there = pl.ds(pl.multiple_of((1 - c) * HD, HD), HD)
+    swap_w = send(remote(w.at[0, :, cols], w.at[1, :, cols], w_ss.at[0], w_rs.at[0], z_peer))
     swap_q = send(remote(q_in.at[away], qp, z_ss.at[0], z_rs.at[0], z_peer))
     swap_do = send(remote(do_in.at[away], dop, z_ss.at[1], z_rs.at[1], z_peer))
-
-    def attend(count, sources, tokens):
-        keys2 = nn(tokens, w[0]).astype(BF16)
-        values2 = nn(tokens, w[1]).astype(BF16)
-        spots = lax.broadcasted_iota(jnp.int32, (32, 128), 0)
-        grads_k, grads_v = [], []
-        for i in range(count):
+    spots = lax.broadcasted_iota(jnp.int32, (32, 128), 0)
+
+    def attend(heads, sources, tokens, first):
+        items = [(h, i) for h in heads for i in range(len(sources))]
+        pairs = {h: nn(tokens, w[h]).astype(BF16) for h in heads}
+        keys = [pairs[h][i * 128 : (i + 1) * 128, :HD] for h, i in items]
+        values = [pairs[h][i * 128 : (i + 1) * 128, HD:] for h, i in items]
+        keeps = [spots < length[zl * NY + src] for src in sources]
+        query, masked = [], []
+        for h, i in items:
             src = sources[i]
-            b = zl * NY + src
-            keep = spots < length[b]
-            both_k, both_v = [], []
-            for h in range(2):
-                query = q[b] if h == 0 else qp[src]
-                cot = do[b] if h == 0 else dop[src]
-                part = slice(i * 128, (i + 1) * 128)
-                cols = slice(h * HD, (h + 1) * HD)
-                key, value = keys2[part, cols], values2[part, cols]
-                scores = nt(query, key) * ROOT
-                top = jnp.max(scores, axis=1, keepdims=True)
-                e = jnp.exp(scores - top)
-                probs = e / jnp.sum(e, axis=1, keepdims=True)
-                probs_b = probs.astype(BF16)
-                out = jnp.where(keep, nn(probs_b, value), 0.0).astype(BF16)
-                masked = jnp.where(keep, cot.astype(F32), 0.0).astype(BF16)
-                both_v.append(tn(probs_b, masked).astype(BF16))
-                grad_probs = nt(masked, value)
-                dots = jnp.sum(probs * grad_probs, axis=1, keepdims=True)
-                grad_scores = (probs * (grad_probs - dots) * ROOT).astype(BF16)
-                grad_q = nn(grad_scores, key).astype(BF16)
-                both_k.append(tn(grad_scores, query).astype(BF16))
-                if h == 0:
-                    att[b] = out
-                    gq[b] = grad_q
-                else:
-                    att_s[src] = out
-                    gq_s[src] = grad_q
-            grads_k.append(jnp.concatenate(both_k, axis=1))
-            grads_v.append(jnp.concatenate(both_v, axis=1))
-        grad_k = grads_k[0] if count == 1 else jnp.concatenate(grads_k, axis=0)
-        grad_v = grads_v[0] if count == 1 else jnp.concatenate(grads_v, axis=0)
-        return grad_k, grad_v
-
-    def pair(dist):
+            query.append(q[zl * NY + src] if h == 0 else qp[src])
+            cot = do[zl * NY + src] if h == 0 else dop[src]
+            masked.append(jnp.where(keeps[i], cot.astype(F32), 0.0).astype(BF16))
+        scores = jnp.concatenate([nt(a, b) for a, b in zip(query, keys)], axis=0) * ROOT
+        grad_probs = jnp.concatenate([nt(a, b) for a, b in zip(masked, values)], axis=0)
+        top = jnp.max(scores, axis=1, keepdims=True)
+        e = jnp.exp(scores - top)
+        probs = e / jnp.sum(e, axis=1, keepdims=True)
+        probs_b = probs.astype(BF16)
+        dots = jnp.sum(probs * grad_probs, axis=1, keepdims=True)
+        grad_scores = (probs * (grad_probs - dots) * ROOT).astype(BF16)
+
+        def rows_of(a, n):
+            return a[n * 32 : (n + 1) * 32]
+
+        outs = [nn(rows_of(probs_b, n), values[n]) for n in range(len(items))]
+        grad_v = [tn(rows_of(probs_b, n), masked[n]).astype(BF16) for n in range(len(items))]
+        grad_q = [nn(rows_of(grad_scores, n), keys[n]).astype(BF16) for n in range(len(items))]
+        grad_k = [tn(rows_of(grad_scores, n), query[n]).astype(BF16) for n in range(len(items))]
+        for n, (h, i) in enumerate(items):
+            out = jnp.where(keeps[i], outs[n], 0.0).astype(BF16)
+            if h == 0:
+                att[zl * NY + sources[i]] = out
+                gq[zl * NY + sources[i]] = grad_q[n]
+            else:
+                out_s[first + i, 0] = out
+                out_s[first + i, 1] = grad_q[n]
+        both = [jnp.concatenate([grad_k[n], grad_v[n]], axis=1) for n in range(len(items))]
+        count = len(sources)
+        grads = [both[n * count : (n + 1) * count] for n in range(len(heads))]
+        return [g[0] if count == 1 else jnp.concatenate(g, axis=0) for g in grads]
+
+    def pair_tokens(dist):
         lo = 2 * (dist - 1)
-        tokens = ring[lo : lo + 2].reshape(256, DI)
-        grad_k, grad_v = attend(2, [y_at(-dist), y_at(dist)], tokens)
-        acc[0] += tn(tokens, grad_k)
-        acc[1] += tn(tokens, grad_v)
+        return ring[lo : lo + 2].reshape(256, DI)
+
+    def pair(dist, heads):
+        tokens = pair_tokens(dist)
+        grads = attend(heads, [y_at(-dist), y_at(dist)], tokens, 2 * dist - 1)
+        if len(heads) == 1:
+            acc[heads[0]] += tn(tokens, grads[0])
+        else:
+            term = tn(tokens, jnp.concatenate(grads, axis=1))
+            acc[0] += term[:, :256]
+            acc[1] += term[:, 256:]
+
+    acc[0] = tn(tok[...], attend((0,), [y], tok[...], 0)[0])
 
     arrive(1, 0)
-    arrive(1, 1)
     for copy in c1:
         copy.wait_recv()
     c2 = send(remote(prow.at[zl], prow.at[zl], c2_ss, c2_rs, z_peer))
+    arrive(1, 1)
     swap_w.wait_recv()
-    share_w = send(remote(w.at[c, :, pl.ds(HD, HD)], w.at[c, :, pl.ds(HD, HD)], w_ss.at[1], w_rs.at[1], c_peer))
+    share_w = send(remote(w.at[1, :, cols], w.at[1, :, cols], w_ss.at[1], w_rs.at[1], c_peer))
+    pair(1, (0,))
 
     arrive(2, 0)
+    c2.wait_recv()
+    pwide[...] = prow[...].reshape(16, 16, 128).astype(F32)
+    part = jnp.zeros((16, HD), F32)
+    for i in range(DI // 128):
+        part += nn(pwide[:, i, :].astype(BF16), wp[i * 128 : (i + 1) * 128, :])
+    gbuf[x, zh, c] = jnp.concatenate([part.astype(BF16), txt[...]], axis=0)
+    c3a = send(remote(gbuf.at[x, zh, c], gbuf.at[x, zh, c], c3_ss.at[0], c3_rs.at[0], c_peer))
     swap_q.wait_recv()
     swap_do.wait_recv()
     share_w.wait_recv()
-    grad_k, grad_v = attend(1, [y], tok[...])
-    acc[0] = tn(tok[...], grad_k)
-    acc[1] = tn(tok[...], grad_v)
-    c2.wait_recv()
-    part = jnp.zeros((16, HD), F32)
-    for i in range(DI // 128):
-        piece = prow[:, :, i, :].reshape(16, 128).astype(BF16)
-        part += nn(piece, wp[i * 128 : (i + 1) * 128, :])
-    gbuf[x, zh, c] = jnp.concatenate([part.astype(BF16), txt[...]], axis=0)
-    c3a = send(remote(gbuf.at[x, zh, c], gbuf.at[x, zh, c], c3_ss.at[0], c3_rs.at[0], c_peer))
+    acc[1] = tn(tok[...], attend((1,), [y], tok[...], 0)[0])
+    pair(1, (1,))
 
     arrive(2, 1)
     c3a.wait_recv()
     c3b = [
         send(remote(gbuf.at[x, zh], gbuf.at[x, zh], c3_ss.at[k], c3_rs.at[k], x_peer(k))) for k in range(1, NX)
     ]
-    pair(1)
+    pair(2, (0, 1))
 
     arrive(3, 0)
     for copy in c3b:
@@ -219,10 +233,10 @@
         send(remote(gbuf.at[:, zh], gbuf.at[:, zh], c3_ss.at[3 + k], c3_rs.at[3 + k], h_peer(k)))
         for k in range(1, NZH)
     ]
-    pair(2)
 
     arrive(3, 1)
-    pair(3)
+    pair(3, (0, 1))
+    back = [send(remote(out_s.at[0:7], out_r.at[0:7], z_ss.at[2], z_rs.at[2], z_peer))]
     for copy in c3c:
         copy.wait_recv()
     every = gbuf[...].reshape(512 // 16, 32, HD)
@@ -251,20 +265,23 @@
     arrive(4, 0)
     arrive(4, 1)
     tokens = ring[6]
-    grad_k, grad_v = attend(1, [y_at(4)], tokens)
+    grads = attend((0, 1), [y_at(4)], tokens, 7)
 
     XR, HR, CR = DI // NX, DI // (NX * NZH), DI // (NX * NZH * NC)
-    theirs = jnp.where(c == 0, grad_v.astype(F32), grad_k.astype(F32)).astype(BF16)
-    ours = jnp.where(c == 0, grad_k.astype(F32), grad_v.astype(F32)).astype(BF16)
+    keys_part = jnp.concatenate([g[:, :HD] for g in grads], axis=1).astype(F32)
+    values_part = jnp.concatenate([g[:, HD:] for g in grads], axis=1).astype(F32)
+    theirs = jnp.where(c == 0, values_part, keys_part).astype(BF16)
+    ours = jnp.where(c == 0, keys_part, values_part).astype(BF16)
     t1 = []
     for i, (lo, hi) in enumerate(((0, 512), (512, 1024), (1024, DI))):
-        s1[lo:hi] = (acc[1 - c, lo:hi] + tn(tokens[:, lo:hi], theirs)).astype(BF16)
+        term = tn(tokens[:, lo:hi], theirs)
+        s1[lo:hi, :HD] = (acc[0, lo:hi, cols_there] + term[:, :HD]).astype(BF16)
+        s1[lo:hi, HD:] = (acc[1, lo:hi, cols_there] + term[:, HD:]).astype(BF16)
         t1.append(send(remote(s1.at[lo:hi], r1.at[lo:hi], t1_ss.at[i], t1_rs.at[i], c_peer)))
-    acc[c] += tn(tokens, ours)
-    back = [
-        send(remote(att_s, att_r, z_ss.at[2], z_rs.at[2], z_peer)),
-        send(remote(gq_s, gq_r, z_ss.at[3], z_rs.at[3], z_peer)),
-    ]
+    back.append(send(remote(out_s.at[7], out_r.at[7], z_ss.at[3], z_rs.at[3], z_peer)))
+    term = tn(tokens, ours)
+    mine[:, :HD] = acc[0, :, cols] + term[:, :HD]
+    mine[:, HD:] = acc[1, :, cols] + term[:, HD:]
     c4.wait_recv()
     for k in range(NY):
         pk2[k] = pk[k] + pz[k]
@@ -291,7 +308,7 @@
     @pl.when(c == 0)
     def _():
         for k in order + (0,):
-            both = acc[0, block(k), :] + r1[block(k), :].astype(F32)
+            both = mine[block(k), :] + r1[block(k), :].astype(F32)
             own2[k] = both[:, :HD]
             s2[k] = both[:, HD:].astype(BF16)
             over_z(k).start()
@@ -299,9 +316,9 @@
     @pl.when(c == 1)
     def _():
         for k in order:
-            s3w[k] = (acc[1, block(k), :] + r1[block(k), :].astype(F32)).astype(BF16)
+            s3w[k] = (mine[block(k), :] + r1[block(k), :].astype(F32)).astype(BF16)
             over_x2(k).start()
-        own_w[...] = acc[1, block(0), :] + r1[block(0), :].astype(F32)
+        own_w[...] = mine[block(0), :] + r1[block(0), :].astype(F32)
 
     total = pk2[y]
     for k in range(1, NY):
@@ -363,8 +380,9 @@
     piece = t3[pl.ds(pl.multiple_of(zh * HR, 8), HR), :]
     for copy in back:
         copy.wait_recv()
-    att[away] = att_r[...]
-    gq[away] = gq_r[...]
+    for i, dist in enumerate((0, -1, 1, -2, 2, -3, 3, 4)):
+        att[(1 - zl) * NY + y_at(dist)] = out_r[i, 0]
+        gq[(1 - zl) * NY + y_at(dist)] = out_r[i, 1]
     answer = cs[...]
     for k in range(1, NY):
         c6[k - 1].wait_recv()
@@ -408,17 +426,15 @@
     hbm = pl.BlockSpec(memory_space=pltpu.HBM)
     dma = pltpu.SemaphoreType.DMA
     V = pltpu.VMEM
-    return pl.pallas_call(
+    ag, dw, con = pl.pallas_call(
         kernel,
         out_shape=(
-            jax.ShapeDtypeStruct((16, 32, HD), BF16),
-            jax.ShapeDtypeStruct((16, 32, HD), BF16),
-            jax.ShapeDtypeStruct((44, HD), F32),
-            jax.ShapeDtypeStruct((44, HD), F32),
+            jax.ShapeDtypeStruct((2, 16, 32, HD), BF16),
+            jax.ShapeDtypeStruct((2, 44, HD), F32),
             jax.ShapeDtypeStruct((2, 16), F32),
         ),
         in_specs=[hbm] * 9 + [smem],
-        out_specs=(vmem,) * 5,
+        out_specs=(vmem,) * 3,
         scratch_shapes=[
             V((128, DI), BF16),
             V((16, 32, HD), BF16),
@@ -432,11 +448,10 @@
             V((2, DI, 256), BF16),
             V((8, 32, HD), BF16),
             V((8, 32, HD), BF16),
-            V((8, 32, HD), BF16),
-            V((8, 32, HD), BF16),
-            V((8, 32, HD), BF16),
-            V((8, 32, HD), BF16),
+            V((8, 2, 32, HD), BF16),
+            V((8, 2, 32, HD), BF16),
             V((2, DI, 256), F32),
+            V((DI, 256), F32),
             V((DI, 256), BF16),
             V((DI, 256), BF16),
             V((4, 352, HD), F32),
@@ -452,7 +467,8 @@
             V((4, 96, HD), BF16),
             V((48, HD), F32),
             V((48, HD), F32),
-            V((2, 8, 16, 128), F32),
+            V((2, 8, 16, 128), BF16),
+            V((16, 16, 128), F32),
             V((4, 4, 2, 32, HD), BF16),
             V((8, 8, 512), F32),
             V((8, 8, 512), F32),
@@ -482,6 +498,7 @@
     )(
         img_tokens.reshape(128, DI), w_key, w_value, queries, lengths, d_out, img_pooled, w_proj, txt_embed, inv_temp
     )
+    return ag[0], ag[1], dw[0], dw[1], con
 
 
 def solution(mesh):

time: 76.8 us -> 73.6 us (0.958)
  Pallas kernels: 70.9 us -> 68.5 us
    unnamed x13 -> x5, local copies, waits for them, and re-layouts: 4.28 us -> 1.23 us
    pallas_call x1, Pallas kernels: 70.9 us -> 68.5 us  [body(): pl.pallas_call(kernel, out_shape=(jax.ShapeDtypeStruct((2, 16, 32, HD), B...]
    squeeze x0 -> x2, local copies, waits for them, and re-layouts: none -> 2.31 us  [body(): return (ag[0], ag[1], dw[0], dw[1], con)]
where the time goes in v3:
time: 73.6 us; the launch traced here: 73.4 us
  Pallas kernels  68.5 us (93%)
  local copies, waits for them, and re-layouts  3.55 us (5%)
  between operations  1.3 us (2%)
    pallas_call x1, Pallas kernels, body(): pl.pallas_call(kernel, out_shape=(jax.ShapeDtypeStruct((2, 16, 32, HD), B...  68.5 us
    squeeze x2, local copies, waits for them, and re-layouts, body(): return (ag[0], ag[1], dw[0], dw[1], con)  2.31 us

profile of v3, /device:TPU:1, one launch (start us, length us, event | category | flops | bytes accessed | tf_op | source)
XLA Modules:
  0.0 73.4 jit_solution(8957108203802430833)
XLA Ops:
  1.3 68.5 %shard_map.137 = (bf16[2,16,32,128]{3,2,1,0:T(8,128)(2,1)}, f32[2,44,128]{2,1,0:T(8,128)}, f32[2,16]{1,0:T(2,128)}) custom-call(bf16[128,1408]{1,0:T(8,128)(2,1)} %bitcast.9, bf16[1408,128]{1,0:T(8,128)(2,1)} %wk.1, bf16[1408,128]{1,0:T(8,128)(2,1)} %wv.1, bf16[16,32,128]{2,1,0:T(8,128)(2,1)} %q_in.1, s32[16]{0:T(128)} %length_in.1, ...), custom_call_target="tpu_custom_call" | custom-call | flops 6200000000 | bytes 4000000 | tf_op jit(solution)/shard_map/pallas_call | solution.py:429
  69.8 0.0 copy-start
  69.8 1.7 %slice_bitcast_fusion = (bf16[16,32,128]{2,1,0:T(8,128)(2,1)}, bf16[16,32,128]{2,1,0:T(8,128)(2,1)}) fusion(bf16[2,16,32,128]{3,2,1,0:T(8,128)(2,1)} %get-tuple-element.8), kind=kLoop, calls=%fused_computation | loop fusion | bytes 524288 | tf_op jit(solution)/shard_map/squeeze | solution.py:501
  71.5 0.0 copy-done
  71.5 0.6 slice_bitcast_fusion.2
  72.2 0.0 copy-start.1
  72.2 0.7 copy-done.1
  72.8 0.6 copy.17
Async XLA Ops:
  69.8 1.7 %copy-start = (f32[2,44,128]{2,1,0:T(8,128)S(1)}, f32[2,44,128]{2,1,0:T(8,128)}, u32[]{:S(2)}) copy-start(f32[2,44,128]{2,1,0:T(8,128)} %get-tuple-element.9) | copy-start | bytes 135172
  72.2 0.7 copy-start.1

commit v4 on v3

--- a/solution.py
+++ b/solution.py
@@ -120,7 +120,7 @@
         )
 
     def arrive(dist, half):
-        for way in (1, -1):
+        for way in (-1, 1):
             if dist < 4 or (half == 0) == (way > 0):
                 hop(way, dist, half).wait_recv()
                 if dist < 3 or (dist == 3 and (half == 0) == (way > 0)):
@@ -273,7 +273,7 @@
     theirs = jnp.where(c == 0, values_part, keys_part).astype(BF16)
     ours = jnp.where(c == 0, keys_part, values_part).astype(BF16)
     t1 = []
-    for i, (lo, hi) in enumerate(((0, 512), (512, 1024), (1024, DI))):
+    for i, (lo, hi) in enumerate(((0, DI),)):
         term = tn(tokens[:, lo:hi], theirs)
         s1[lo:hi, :HD] = (acc[0, lo:hi, cols_there] + term[:, :HD]).astype(BF16)
         s1[lo:hi, HD:] = (acc[1, lo:hi, cols_there] + term[:, HD:]).astype(BF16)
@@ -485,7 +485,7 @@
             dma, dma,
             dma((8,)), dma((8,)),
             dma((8,)), dma((8,)),
-            dma((3,)), dma((3,)),
+            dma((1,)), dma((1,)),
             dma((4,)), dma((4,)),
             dma((4,)), dma((4,)),
             dma((4,)), dma((4,)),

time: 73.6 us -> 73.6 us (level)
  no operation moved by 1% of the time
where the time goes in v4:
time: 73.6 us; the launch traced here: 73.4 us
  Pallas kernels  68.5 us (93%)
  local copies, waits for them, and re-layouts  3.55 us (5%)
  between operations  1.3 us (2%)
    pallas_call x1, Pallas kernels, body(): pl.pallas_call(kernel, out_shape=(jax.ShapeDtypeStruct((2, 16, 32, HD), B...  68.5 us
    squeeze x2, local copies, waits for them, and re-layouts, body(): return (ag[0], ag[1], dw[0], dw[1], con)  2.31 us

profile of v4, /device:TPU:1, one launch (start us, length us, event | category | flops | bytes accessed | tf_op | source)
XLA Modules:
  0.0 73.4 jit_solution(10179525556292897190)
XLA Ops:
  1.3 68.5 %shard_map.137 = (bf16[2,16,32,128]{3,2,1,0:T(8,128)(2,1)}, f32[2,44,128]{2,1,0:T(8,128)}, f32[2,16]{1,0:T(2,128)}) custom-call(bf16[128,1408]{1,0:T(8,128)(2,1)} %bitcast.9, bf16[1408,128]{1,0:T(8,128)(2,1)} %wk.1, bf16[1408,128]{1,0:T(8,128)(2,1)} %wv.1, bf16[16,32,128]{2,1,0:T(8,128)(2,1)} %q_in.1, s32[16]{0:T(128)} %length_in.1, ...), custom_call_target="tpu_custom_call" | custom-call | flops 6200000000 | bytes 4000000 | tf_op jit(solution)/shard_map/pallas_call | solution.py:429
  69.8 0.0 copy-start
  69.8 1.7 %slice_bitcast_fusion = (bf16[16,32,128]{2,1,0:T(8,128)(2,1)}, bf16[16,32,128]{2,1,0:T(8,128)(2,1)}) fusion(bf16[2,16,32,128]{3,2,1,0:T(8,128)(2,1)} %get-tuple-element.8), kind=kLoop, calls=%fused_computation | loop fusion | bytes 524288 | tf_op jit(solution)/shard_map/squeeze | solution.py:501
  71.5 0.0 copy-done
  71.5 0.6 slice_bitcast_fusion.2
  72.2 0.0 copy-start.1
  72.2 0.7 copy-done.1
  72.8 0.6 copy.17
Async XLA Ops:
  69.8 1.7 %copy-start = (f32[2,44,128]{2,1,0:T(8,128)S(1)}, f32[2,44,128]{2,1,0:T(8,128)}, u32[]{:S(2)}) copy-start(f32[2,44,128]{2,1,0:T(8,128)} %get-tuple-element.9) | copy-start | bytes 135172
  72.2 0.7 copy-start.1
